TPU v7x, 32 devices: a whole 2x2x4 slice. The times are simulated.
32 devices in a mesh: sfc: 32 (over z, y, x, core).
Axes of the slice: x: 2, y: 2, z: 4, core: 2. Of those that a mesh axis runs over, the one named last changes fastest.
Arguments:
- state: float32 [5, 2048, 512], P(None, 'sfc'), may hold values from -0.47 to 4.3, as said below
- volume: int32 [2048, 512], P('sfc'), may hold values from 1 to 8, as said below
- neighbour: int32 [2048, 6], P('sfc'), may hold values from -1 to 2047, as said below
- parent: int32 [2048], P('sfc'), may hold values from 0 to 2047, as said below
Outputs:
- fine_state: float32 [5, 2048, 512], P(None, 'sfc')
- coarse_state: float32 [5, 256, 512], P(None, 'sfc')
- coarse_residual: float32 [5, 256, 512], P(None, 'sfc')
Inputs may be any that keep to these rules, and one draw needn't show every extreme that they name: `state`: each cell has density 0.65 to 1.55, x velocity 0.2 to 0.8, y and z velocity of size 0.3 at most, pressure 0.55 to 1.45, and total energy = pressure / 0.4 + half the density times the squared speed. `volume`: every cell of a brick that is not cut holds 8; a cut brick has some cell under 8. One device's 64 bricks hold at most 16 cut bricks, and some device holds exactly 16. `neighbour`: the fine bricks form a grid of 16 x 16 x 8, periodic along y, with -1 on the far-field faces at the ends of x and z. The grid is cut into cubes of 4 x 4 x 4 bricks, ordered along a Morton curve: device d holds the cube whose coordinates (in cubes) have bit i // 3 of x, y or z equal to bit i of d, as i % 3 is 0, 1 or 2, as bricks d * 64 to (d + 1) * 64 - 1 in no particular order. The relation is symmetric. `parent`: every pair of a coarse brick and an octant occurs exactly once; the octant gives the parities of the fine brick's x, y and z positions. The coarse level is the fine grid halved, ordered along its own Morton curve and cut into runs of 8 that start half a run later than the fine level's cuts: coarse brick c is held by device c // 8, and of each device's fine bricks exactly 32 have their parents on the next device (the last device's on device 0) and the rest on the device itself.
All inputs are finite; a program needn't handle non-finite values.
Results may differ from a plain program's by a relative error of at most 0.00002.
Values sent between devices are 32-bit elements; how exact they have to be, the bound alone decides.
A program may use at most 128 MiB of HBM per device.

v0:
```python
import functools

import jax
import jax.numpy as jnp
from jax import lax
from jax.experimental import pallas as pl
from jax.experimental.pallas import tpu as pltpu
from jax.sharding import PartitionSpec as P

BE = 8
CUBE = 4
LANES = 128
CFL_NUMBER = 0.25
FIRST_SECTION = 0.5
STREAM = (1.0, 0.5, 0.0, 0.0, 1.0 / (1.4 * (1.4 - 1.0)) + 0.125)
f32 = jnp.float32
bf16 = jnp.bfloat16
i32 = jnp.int32
MESH = pl.DeviceIdType.MESH


def iota(shape, dim):
    return lax.broadcasted_iota(i32, shape, dim)


def pieces(x):
    hi = x.astype(bf16)
    rest = x - hi.astype(f32)
    mid = rest.astype(bf16)
    low = (rest - mid.astype(f32)).astype(bf16)
    return hi, mid, low


def dot(a, b, dims):
    return lax.dot_general(a, b, (dims, ((), ())), preferred_element_type=f32)


def prims(u):
    inv = 1.0 / u[0]
    vel = [u[1] * inv, u[2] * inv, u[3] * inv]
    kinetic = 0.5 * (u[1] * vel[0] + u[2] * vel[1] + u[3] * vel[2])
    pressure = 0.4 * (u[4] - kinetic)
    sound = jnp.sqrt(1.4 * pressure * inv)
    return vel, pressure, sound


def flux(u, v, p, k):
    out = [u[1 + k]]
    for j in range(3):
        m = u[1 + j] * v
        out.append(m + p if j == k else m)
    out.append((u[4] + p) * v)
    return out


def face(ul, vl, pl_, sl, al, ur, vr, pr, sr, ar, k, mask):
    s = jnp.maximum(sl, sr)
    a = jnp.minimum(al, ar)
    if mask is not None:
        a = jnp.where(mask, a, 0.0)
    half = 0.5 * a
    fl = flux(ul, vl, pl_, k)
    fr = flux(ur, vr, pr, k)
    w = [half * ((fl[i] + fr[i]) - s * (ur[i] - ul[i])) for i in range(5)]
    return w, a * s


def face_from(ul, al, ur, ar, k, mask=None):
    vl, pl_, cl = prims(ul)
    vr, pr, cr = prims(ur)
    return face(ul, vl[k], pl_, jnp.abs(vl[k]) + cl, al,
                ur, vr[k], pr, jnp.abs(vr[k]) + cr, ar, k, mask)


def roll(x, shift, axis):
    size = x.shape[axis]
    shift = shift % size
    return x if shift == 0 else pltpu.roll(x, shift, axis)


def kernel(n, vol_ref, nb_ref, par_ref, x_ref,
           fine_ref, cs_ref, cr_ref,
           u0, u1, res, lam, box, gain, frac_send, send, recv, csend, crecv,
           ssem, rsem, cssem, crsem):
    me = lax.axis_index("sfc")
    bits = n.bit_length() - 1
    brick = x_ref.shape[1]
    cells = BE ** 3

    coord, extent = [], []
    for k in range(3):
        value, size = 0, 1
        for i in range(bits):
            if i % 3 == k:
                value = value + (me // (1 << i)) % 2 * size
                size *= 2
        coord.append(value)
        extent.append(size)

    def device_at(axis, value):
        out = 0
        for i in range(bits):
            k = i % 3
            source = value if k == axis else coord[k]
            out = out + (source // (1 << (i // 3))) % 2 * (1 << i)
        return out

    below = [device_at(k, (coord[k] + extent[k] - 1) % extent[k]) for k in range(3)]
    above = [device_at(k, (coord[k] + 1) % extent[k]) for k in range(3)]
    nxt, prev = (me + 1) % n, (me + n - 1) % n

    barrier = pltpu.get_barrier_semaphore()
    for target in below + above + [nxt, prev]:
        pl.semaphore_signal(barrier, inc=1, device_id=(target,), device_id_type=MESH)

    nb = nb_ref[...]
    par = par_ref[...].astype(f32)
    eye = iota((brick, brick), 0) == iota((brick, brick), 1)
    par_col = jnp.sum(jnp.where(eye, par, 0.0), axis=1, keepdims=True)
    par_int = par_col.astype(i32)
    octant = par_int & 7
    remote = jnp.where((nb < 0) | (lax.div(jnp.maximum(nb, 0), brick) != me), 1, 0)

    def position(axis, parity):
        low = remote[:, 2 * axis:2 * axis + 1]
        high = remote[:, 2 * axis + 1:2 * axis + 2]
        return jnp.where(parity == 0, 2 - 2 * low, 1 + 2 * high)

    bx = position(0, octant >> 2)
    by = position(1, (octant >> 1) & 1)
    bz = position(2, octant & 1)
    lane0 = bx * 32 + by * 4 + bz
    lane2 = jnp.concatenate([lane0, lane0 + 16], axis=0)
    hot = iota((2 * brick, LANES), 1) == lane2
    perm = jnp.where(hot, 1.0, 0.0).astype(bf16)
    par_lane = jnp.sum(jnp.where(hot, jnp.concatenate([par_col, par_col], axis=0), 0.0),
                       axis=0, keepdims=True).astype(i32)

    def to_grid(x):
        both = jnp.concatenate([x[:, :cells // 2], x[:, cells // 2:]], axis=0)
        return both

    def put(f, parts):
        total = sum(dot(part, perm, ((0,), (0,))) for part in parts)
        u0[f] = total.reshape(4, 8, 8, LANES)

    put(5, [(to_grid(vol_ref[...]).astype(f32) * 0.125).astype(bf16)])
    for f in range(5):
        put(f, pieces(to_grid(x_ref[f])))

    lane = iota((1, 1, LANES), 2)
    block_x, lane_by, lane_bz = lane >> 4, (lane >> 2) & 3, lane & 3
    ixhi = (lane >> 4) & 1
    iz = iota((1, 8, LANES), 1)
    lane_l = iota((1, 8, LANES), 2)

    slot_of = (block_x, lane_by, lane_bz)
    packed_slots = (8, 4, 4)

    def source_layer(src, count, k, high, j):
        if k == 0:
            return src[0:count, 3 if high else 0, j]
        if k == 1:
            return src[0:count, j, 7 if high else 0]
        z = 7 if high else 0
        return src[0:count, j, :, z, :]

    strides = (16, 4, 1)

    def pack(src, count, k, high):
        total = None
        last = packed_slots[k] - 1
        for j in range(packed_slots[k]):
            v = source_layer(src, count, k, high, j)
            v = roll(v, strides[k] * (j - (last if high else 0)), 2)
            total = v if total is None else jnp.where(slot_of[k] == j, v, total)
        return total

    def unpack(w, k, high, j):
        last = packed_slots[k] - 1
        v = roll(w, strides[k] * ((last if high else 0) - j), w.ndim - 1)
        return v

    def exchange(stage, src):
        copies = []
        count = 6 if stage == 0 else 5
        for k in range(3):
            for high in (0, 1):
                face_index = 2 * k + high
                send[stage, face_index, 0:count] = pack(src, count, k, high)
        if stage == 0:
            pl.semaphore_wait(barrier, 8)
        for k in range(3):
            for high in (0, 1):
                mine = 2 * k + high
                copy = pltpu.make_async_remote_copy(
                    src_ref=send.at[stage, mine, pl.ds(0, count)],
                    dst_ref=recv.at[stage, 2 * k + 1 - high, pl.ds(0, count)],
                    send_sem=ssem.at[stage, mine],
                    recv_sem=rsem.at[stage, 2 * k + 1 - high],
                    device_id=((above if high else below)[k],),
                    device_id_type=MESH,
                )
                copy.start()
                copies.append(copy)
        return copies

    def shift_x(a):
        return jnp.concatenate([a[1:4], roll(a[0:1], -16, 2)], axis=0)

    def back_x(a):
        return jnp.concatenate([roll(a[3:4], 16, 2), a[0:3]], axis=0)

    def shift_y(a):
        return jnp.concatenate([a[1:8], roll(a[0:1], -4, 2)], axis=0)

    def back_y(a):
        return jnp.concatenate([roll(a[7:8], 4, 2), a[0:7]], axis=0)

    def shift_z(a):
        b = roll(a, -1, 1)
        return jnp.where(iz == 7, roll(b, -1, 2), b)

    def back_z(a):
        b = roll(a, 1, 1)
        return jnp.where(iz == 0, roll(b, 1, 2), b)

    slab = iota((4, 1, LANES), 0)
    mask_x = jnp.logical_not((slab == 3) & (block_x == 7))
    row = iota((8, 1, LANES), 0)
    mask_y = jnp.logical_not((row == 7) & (lane_by == 3))
    mask_z = jnp.logical_not((iz == 7) & ((lane_l & 3) == 3))

    def interior(src, want_lam):
        def pass_xz(y, carry):
            u = [src[f, :, y] for f in range(5)]
            a = u0[5, :, y]
            vel, p, c = prims(u)
            total = spread = None
            for k, ahead, back, mask in ((0, shift_x, back_x, mask_x), (2, shift_z, back_z, mask_z)):
                speed = jnp.abs(vel[k]) + c
                w, s = face(u, vel[k], p, speed, a,
                            [ahead(q) for q in u], ahead(vel[k]), ahead(p), ahead(speed), ahead(a),
                            k, mask)
                diff = [q - back(q) for q in w]
                total = diff if total is None else [t + d for t, d in zip(total, diff)]
                if want_lam:
                    both = s + back(s)
                    spread = both if spread is None else spread + both
            for f in range(5):
                res[f, :, y] = total[f]
            if want_lam:
                lam[:, y] = spread
            return carry

        lax.fori_loop(0, 8, pass_xz, 0)

        def pass_y(x, carry):
            u = [src[f, x] for f in range(5)]
            a = u0[5, x]
            vel, p, c = prims(u)
            speed = jnp.abs(vel[1]) + c
            w, s = face(u, vel[1], p, speed, a,
                        [shift_y(q) for q in u], shift_y(vel[1]), shift_y(p), shift_y(speed), shift_y(a),
                        1, mask_y)
            for f in range(5):
                res[f, x] = res[f, x] + (w[f] - back_y(w[f]))
            if want_lam:
                lam[x] = lam[x] + (s + back_y(s))
            return carry

        lax.fori_loop(0, 4, pass_y, 0)

    def boundary(stage, copies, want_lam):
        for copy in copies:
            copy.wait()
        for k in range(3):
            for high in (0, 1):
                index = 2 * k + high
                own_u = [send[stage, index, f] for f in range(5)]
                own_a = send[0, index, 5]
                other_u = [recv[stage, index, f] for f in range(5)]
                other_a = recv[0, index, 5]
                if k != 1:
                    at_end = coord[k] == (extent[k] - 1 if high else 0)
                    other_u = [jnp.where(at_end, STREAM[f], other_u[f]) for f in range(5)]
                    other_a = jnp.where(at_end, own_a, other_a)
                if high:
                    w, s = face_from(own_u, own_a, other_u, other_a, k)
                    sign = 1.0
                else:
                    w, s = face_from(other_u, other_a, own_u, own_a, k)
                    sign = -1.0
                edge = packed_slots[k] - 1 if high else 0
                values = jnp.stack([sign * q for q in w] + ([s] if want_lam else []), axis=0)
                here = slot_of[k] == edge
                for j in range(packed_slots[k]):
                    add = jnp.where(here, unpack(values, k, high, j), 0.0)
                    if k == 0:
                        at = (3 if high else 0, j)
                    elif k == 1:
                        at = (j, 7 if high else 0)
                    else:
                        at = (j, slice(None), 7 if high else 0, slice(None))
                    where5 = (slice(0, 5),) + at
                    res[where5] = res[where5] + add[0:5]
                    if want_lam:
                        lam[at] = lam[at] + add[5]

    def box_x(a):
        up = jnp.where(ixhi == 0, roll(a[0:1], -16, 2), 0.0)
        down = jnp.where(ixhi == 1, roll(a[3:4], 16, 2), 0.0)
        return a + jnp.concatenate([a[1:4], up], axis=0) + jnp.concatenate([down, a[0:3]], axis=0)

    def box_y(a):
        zero = jnp.zeros_like(a[0:1])
        return a + jnp.concatenate([a[1:8], zero], axis=0) + jnp.concatenate([zero, a[0:7]], axis=0)

    def box_z(a):
        return a + jnp.where(iz == 7, 0.0, roll(a, -1, 1)) + jnp.where(iz == 0, 0.0, roll(a, 1, 1))

    def box_of_frac():
        def first(y, carry):
            box[0, :, y] = box_z(box_x(u0[5, :, y]))
            return carry
        lax.fori_loop(0, 8, first, 0)

        def second(x, carry):
            gain[x] = (1.0 - u0[5, x]) / box_y(box[0, x])
            return carry
        lax.fori_loop(0, 4, second, 0)

    def update(factor):
        def first(y, carry):
            share = u0[5, :, y] * (-CFL_NUMBER / lam[:, y])
            for f in range(5):
                d = share * res[f, :, y]
                res[f, :, y] = d
                box[f, :, y] = box_z(box_x(d))
            return carry
        lax.fori_loop(0, 8, first, 0)

        def second(x, carry):
            g = gain[x]
            for f in range(5):
                u1[f, x] = u0[f, x] + factor * (res[f, x] + g * box_y(box[f, x]))
            return carry
        lax.fori_loop(0, 4, second, 0)

    copies0 = exchange(0, u0)
    box_of_frac()
    interior(u0, True)
    boundary(0, copies0, True)
    update(FIRST_SECTION)

    copies1 = exchange(1, u1)
    interior(u1, True)
    boundary(1, copies1, True)
    update(1.0)

    copies2 = exchange(2, u1)

    c = iota((LANES, 256), 0)
    col = iota((LANES, 256), 1)
    rowc = col & 63
    spread = (((c >> 6) == (rowc >> 5)) & (((c >> 3) & 3) == ((rowc >> 3) & 3))
              & ((rowc & 7) == 2 * (c & 3))
              & (((c >> 5) & 1) == (col >> 7)) & (((c >> 2) & 1) == ((col >> 6) & 1)))
    spread = jnp.where(spread, 1.0, 0.0).astype(bf16)
    r = iota((64, LANES), 0)
    ln = iota((64, LANES), 1)
    coarse_base = jnp.where(r >= 32, nxt, me) * (brick // 8)
    pick = ((((r >> 3) & 3) == ((ln >> 4) & 3))
            & (jnp.broadcast_to(par_lane >> 3, (64, LANES)) == coarse_base + (r & 7)))
    pick = jnp.where(pick, 1.0, 0.0).astype(bf16)
    lane2d = iota((1, LANES), 1)
    which = ((lane2d >> 2) & 1) * 2 + (lane2d & 1)

    def sums(x):
        g = x.reshape(2, 2, 4, 2, 8, LANES)
        s = (g[:, 0, :, 0] + g[:, 0, :, 1]) + (g[:, 1, :, 0] + g[:, 1, :, 1])
        s = s.reshape(8, 8, LANES)
        return s + roll(s, -1, 1)

    def place(s):
        flat = s.reshape(64, LANES)
        stacked = jnp.concatenate([jnp.where(which == o, flat, 0.0) for o in range(4)], axis=0)
        z = sum(dot(spread, part, ((1,), (0,))) for part in pieces(stacked))
        return sum(dot(pick, part, ((1,), (1,))) for part in pieces(z))

    def coarse(group, f, s, out):
        placed = place(s)
        csend[group, f] = placed[32:64]
        for t in range(4):
            out[f, :, t * LANES:(t + 1) * LANES] = placed[8 * t:8 * t + 8]

    def coarse_copy(group):
        copy = pltpu.make_async_remote_copy(
            src_ref=csend.at[group], dst_ref=crecv.at[group],
            send_sem=cssem.at[group], recv_sem=crsem.at[group],
            device_id=(nxt,), device_id_type=MESH)
        copy.start()
        return copy

    def coarse_finish(group, copy, out):
        copy.wait()
        for f in range(5):
            for t in range(4):
                at = (f, slice(None), slice(t * LANES, (t + 1) * LANES))
                out[at] = out[at] + crecv[group, f, 8 * t:8 * t + 8]

    inv = 1.0 / sums(u0[5])
    for f in range(5):
        coarse(0, f, sums(u0[5] * u1[f]) * inv, cs_ref)
    state_copy = coarse_copy(0)

    interior(u1, False)

    boundary(2, copies2, False)
    for f in range(5):
        coarse(1, f, sums(res[f]), cr_ref)
    residual_copy = coarse_copy(1)

    for f in range(5):
        flat = u1[f].reshape(256, LANES)
        back = sum(dot(perm, part, ((1,), (1,))) for part in pieces(flat))
        fine_ref[f, :, 0:256] = back[0:brick]
        fine_ref[f, :, 256:512] = back[brick:2 * brick]

    coarse_finish(0, state_copy, cs_ref)
    coarse_finish(1, residual_copy, cr_ref)


def local(n, state, volume, neighbour, parent):
    brick = state.shape[1]
    grid = (4, 8, 8, LANES)
    vmem = pl.BlockSpec(memory_space=pltpu.VMEM)
    coarse_shape = jax.ShapeDtypeStruct((5, brick // 8, BE ** 3), f32)
    return pl.pallas_call(
        functools.partial(kernel, n),
        out_shape=(jax.ShapeDtypeStruct(state.shape, f32), coarse_shape, coarse_shape),
        in_specs=[vmem] * 4,
        out_specs=(vmem,) * 3,
        scratch_shapes=[
            pltpu.VMEM((6,) + grid, f32),
            pltpu.VMEM((5,) + grid, f32),
            pltpu.VMEM((5,) + grid, f32),
            pltpu.VMEM(grid, f32),
            pltpu.VMEM((5,) + grid, f32),
            pltpu.VMEM(grid, f32),
            pltpu.VMEM((8, LANES), f32),
            pltpu.VMEM((3, 6, 6, 8, LANES), f32),
            pltpu.VMEM((3, 6, 6, 8, LANES), f32),
            pltpu.VMEM((2, 5, 32, LANES), f32),
            pltpu.VMEM((2, 5, 32, LANES), f32),
            pltpu.SemaphoreType.DMA((3, 6)),
            pltpu.SemaphoreType.DMA((3, 6)),
            pltpu.SemaphoreType.DMA((2,)),
            pltpu.SemaphoreType.DMA((2,)),
        ],
        compiler_params=pltpu.CompilerParams(
            collective_id=0, has_side_effects=True, vmem_limit_bytes=40 * 1024 * 1024),
    )(volume, neighbour, parent.reshape(1, brick), state)


def solution(mesh):
    in_specs = (P(None, "sfc", None), P("sfc", None), P("sfc", None), P("sfc"))
    out_specs = (P(None, "sfc", None), P(None, "sfc", None), P(None, "sfc", None))
    return jax.shard_map(functools.partial(local, mesh.shape["sfc"]), mesh=mesh,
                         in_specs=in_specs, out_specs=out_specs, check_vma=False)
```

profile of v0, /device:TPU:0, one launch (start us, length us, event | category | flops | bytes accessed | tf_op | source)
XLA Modules:
  0.0 31.9 jit_solution(4895769460144904596)
XLA Ops:
  0.6 0.0 copy-start.2
  0.6 0.8 %copy.7.nb_ref = s32[64,6]{1,0:T(8,128)S(1)} copy(s32[64,6]{0,1:T(8,128)} %param.6) | data formatting | bytes 3072 | tf_op args[2]
  1.4 0.0 copy-done.2
  1.4 0.0 copy-start
  1.4 1.1 %copy-done = f32[5,64,512]{2,1,0:T(8,128)S(1)} copy-done((f32[5,64,512]{2,1,0:T(8,128)S(1)}, f32[5,64,512]{2,1,0:T(8,128)}, u32[]{:S(2)}) %copy-start) | copy-done | bytes 655384
  2.5 0.0 copy-start.1
  2.5 0.9 %copy-done.1 = s32[64,512]{1,0:T(8,128)S(1)} copy-done((s32[64,512]{1,0:T(8,128)S(1)}, s32[64,512]{1,0:T(8,128)}, u32[]{:S(2)}) %copy-start.1) | copy-done | bytes 131096
  3.4 26.3 %shard_map.67 = (f32[5,64,512]{2,1,0:T(8,128)S(1)}, f32[5,8,512]{2,1,0:T(8,128)S(1)}, f32[5,8,512]{2,1,0:T(8,128)S(1)}) custom-call(s32[64,512]{1,0:T(8,128)S(1)} %copy-done.1, s32[64,6]{1,0:T(8,128)S(1)} %copy.7.nb_ref, s32[1,64]{1,0:T(1,128)S(1)} %bitcast.1, f32[5,64,512]{2,1,0:T(8,128)S(1)} %copy-done), custom_call_target="tpu_custom_call" | custom-call | tf_op jit(solution)/shard_map/pallas_call | solution.py:439
  29.7 0.8 %copy.11 = f32[5,64,512]{2,1,0:T(8,128)} copy(f32[5,64,512]{2,1,0:T(8,128)S(1)} %get-tuple-element.6) | data formatting | bytes 1310720
  30.6 0.6 %copy.12 = f32[5,8,512]{2,1,0:T(8,128)} copy(f32[5,8,512]{2,1,0:T(8,128)S(1)} %get-tuple-element.7) | data formatting | bytes 163840
  31.2 0.6 %copy.13 = f32[5,8,512]{2,1,0:T(8,128)} copy(f32[5,8,512]{2,1,0:T(8,128)S(1)} %get-tuple-element.8) | data formatting | bytes 163840
Async XLA Ops:
  0.6 0.8 %copy-start.2 = (s32[64]{0:T(128)S(1)}, s32[64]{0:T(128)}, u32[]{:S(2)}) copy-start(s32[64]{0:T(128)} %param.7) | copy-start | bytes 772
  1.4 1.1 %copy-start = (f32[5,64,512]{2,1,0:T(8,128)S(1)}, f32[5,64,512]{2,1,0:T(8,128)}, u32[]{:S(2)}) copy-start(f32[5,64,512]{2,1,0:T(8,128)} %x_ref.1) | copy-start | bytes 1966084
  2.5 0.9 %copy-start.1 = (s32[64,512]{1,0:T(8,128)S(1)}, s32[64,512]{1,0:T(8,128)}, u32[]{:S(2)}) copy-start(s32[64,512]{1,0:T(8,128)} %vol_ref.1) | copy-start | bytes 393220
where the time goes:
time: 32.1 us; the launch traced here: 31.9 us
  Pallas kernels  26.3 us (82%)
  local copies, waits for them, and re-layouts  4.88 us (15%)
  between operations  0.66 us (2%)
    pallas_call x1, Pallas kernels, local(): pl.pallas_call(functools.partial(kernel, n), out_shape=(jax.ShapeDtypeStr...  26.3 us
    unnamed x10, local copies, waits for them, and re-layouts  4.88 us

commit v1 on v0

--- a/solution.py
+++ b/solution.py
@@ -78,14 +78,20 @@
     return x if shift == 0 else pltpu.roll(x, shift, axis)
 
 
-def kernel(n, vol_ref, nb_ref, par_ref, x_ref,
+def kernel(n, vol_hbm, nb_ref, par_ref, x_hbm,
            fine_ref, cs_ref, cr_ref,
-           u0, u1, res, lam, box, gain, frac_send, send, recv, csend, crecv,
+           vol_ref, x_ref, in_sem, u0, u1, res, lam, box, gain, send, recv, csend, crecv,
            ssem, rsem, cssem, crsem):
     me = lax.axis_index("sfc")
     bits = n.bit_length() - 1
     brick = x_ref.shape[1]
     cells = BE ** 3
+
+    loads = [pltpu.make_async_copy(vol_hbm, vol_ref, in_sem.at[5])]
+    for f in range(5):
+        loads.append(pltpu.make_async_copy(x_hbm.at[f], x_ref.at[f], in_sem.at[f]))
+    for load in loads:
+        load.start()
 
     coord, extent = [], []
     for k in range(3):
@@ -114,22 +120,25 @@
         pl.semaphore_signal(barrier, inc=1, device_id=(target,), device_id_type=MESH)
 
     nb = nb_ref[...]
-    par = par_ref[...].astype(f32)
-    eye = iota((brick, brick), 0) == iota((brick, brick), 1)
-    par_col = jnp.sum(jnp.where(eye, par, 0.0), axis=1, keepdims=True)
-    par_int = par_col.astype(i32)
-    octant = par_int & 7
+    par = par_ref[...]
+    octant = par & 7
     remote = jnp.where((nb < 0) | (lax.div(jnp.maximum(nb, 0), brick) != me), 1, 0)
 
     def position(axis, parity):
-        low = remote[:, 2 * axis:2 * axis + 1]
-        high = remote[:, 2 * axis + 1:2 * axis + 2]
+        low = remote[2 * axis:2 * axis + 1]
+        high = remote[2 * axis + 1:2 * axis + 2]
         return jnp.where(parity == 0, 2 - 2 * low, 1 + 2 * high)
 
     bx = position(0, octant >> 2)
     by = position(1, (octant >> 1) & 1)
     bz = position(2, octant & 1)
-    lane0 = bx * 32 + by * 4 + bz
+    eye = iota((brick, brick), 0) == iota((brick, brick), 1)
+
+    def column(r):
+        return jnp.sum(jnp.where(eye, r.astype(f32), 0.0), axis=1, keepdims=True)
+
+    par_col = column(par)
+    lane0 = column(bx * 32 + by * 4 + bz).astype(i32)
     lane2 = jnp.concatenate([lane0, lane0 + 16], axis=0)
     hot = iota((2 * brick, LANES), 1) == lane2
     perm = jnp.where(hot, 1.0, 0.0).astype(bf16)
@@ -140,13 +149,16 @@
         both = jnp.concatenate([x[:, :cells // 2], x[:, cells // 2:]], axis=0)
         return both
 
-    def put(f, parts):
-        total = sum(dot(part, perm, ((0,), (0,))) for part in parts)
+    perm2 = jnp.concatenate([perm, perm], axis=0)
+    loads[0].wait()
+    volume = (to_grid(vol_ref[...]).astype(f32) * 0.125).astype(bf16)
+    u0[5] = dot(volume, perm, ((0,), (0,))).reshape(4, 8, 8, LANES)
+    for f in range(5):
+        loads[1 + f].wait()
+        hi, mid, low = pieces(to_grid(x_ref[f]))
+        total = (dot(jnp.concatenate([hi, mid], axis=0), perm2, ((0,), (0,)))
+                 + dot(low, perm, ((0,), (0,))))
         u0[f] = total.reshape(4, 8, 8, LANES)
-
-    put(5, [(to_grid(vol_ref[...]).astype(f32) * 0.125).astype(bf16)])
-    for f in range(5):
-        put(f, pieces(to_grid(x_ref[f])))
 
     lane = iota((1, 1, LANES), 2)
     block_x, lane_by, lane_bz = lane >> 4, (lane >> 2) & 3, lane & 3
@@ -360,21 +372,16 @@
 
     copies2 = exchange(2, u1)
 
-    c = iota((LANES, 256), 0)
-    col = iota((LANES, 256), 1)
-    rowc = col & 63
-    spread = (((c >> 6) == (rowc >> 5)) & (((c >> 3) & 3) == ((rowc >> 3) & 3))
-              & ((rowc & 7) == 2 * (c & 3))
-              & (((c >> 5) & 1) == (col >> 7)) & (((c >> 2) & 1) == ((col >> 6) & 1)))
-    spread = jnp.where(spread, 1.0, 0.0).astype(bf16)
     r = iota((64, LANES), 0)
     ln = iota((64, LANES), 1)
     coarse_base = jnp.where(r >= 32, nxt, me) * (brick // 8)
     pick = ((((r >> 3) & 3) == ((ln >> 4) & 3))
             & (jnp.broadcast_to(par_lane >> 3, (64, LANES)) == coarse_base + (r & 7)))
     pick = jnp.where(pick, 1.0, 0.0).astype(bf16)
-    lane2d = iota((1, LANES), 1)
-    which = ((lane2d >> 2) & 1) * 2 + (lane2d & 1)
+    pick2 = jnp.concatenate([pick, pick], axis=1)
+    lane_oy, lane_oz = (lane >> 2) & 1, lane & 1
+    sub = iota((1, 8, LANES), 1)
+    same_oz = (sub >> 2) == lane_oz
 
     def sums(x):
         g = x.reshape(2, 2, 4, 2, 8, LANES)
@@ -382,17 +389,25 @@
         s = s.reshape(8, 8, LANES)
         return s + roll(s, -1, 1)
 
-    def place(s):
-        flat = s.reshape(64, LANES)
-        stacked = jnp.concatenate([jnp.where(which == o, flat, 0.0) for o in range(4)], axis=0)
-        z = sum(dot(spread, part, ((1,), (0,))) for part in pieces(stacked))
-        return sum(dot(pick, part, ((1,), (1,))) for part in pieces(z))
-
-    def coarse(group, f, s, out):
-        placed = place(s)
-        csend[group, f] = placed[32:64]
-        for t in range(4):
-            out[f, :, t * LANES:(t + 1) * LANES] = placed[8 * t:8 * t + 8]
+    def coarse_rows(s):
+        t = s
+        for j in range(1, 4):
+            t = jnp.where(sub == j, roll(s, -j, 1), t)
+        t = jnp.where(sub >= 4, roll(t, 4, 1), t)
+        t = jnp.where(same_oz, t, 0.0)
+        both = [jnp.where(lane_oy == oy, t, 0.0) for oy in range(2)]
+        return jnp.concatenate([both[0][0:4], both[1][0:4], both[0][4:8], both[1][4:8]],
+                               axis=0).reshape(LANES, LANES)
+
+    def coarse(group, values, out):
+        z = jnp.concatenate([coarse_rows(s) for s in values], axis=0)
+        hi, mid, _ = pieces(z)
+        placed = dot(pick2, jnp.concatenate([hi, mid], axis=1), ((1,), (1,)))
+        for f in range(5):
+            block = placed[:, f * LANES:(f + 1) * LANES]
+            csend[group, f] = block[32:64]
+            for t in range(4):
+                out[f, :, t * LANES:(t + 1) * LANES] = block[8 * t:8 * t + 8]
 
     def coarse_copy(group):
         copy = pltpu.make_async_remote_copy(
@@ -410,45 +425,57 @@
                 out[at] = out[at] + crecv[group, f, 8 * t:8 * t + 8]
 
     inv = 1.0 / sums(u0[5])
+    coarse(0, [sums(u0[5] * u1[f]) * inv for f in range(5)], cs_ref)
+    state_copy = coarse_copy(0)
+
+    interior(u1, False)
+
+    boundary(2, copies2, False)
+    coarse(1, [sums(res[f]) for f in range(5)], cr_ref)
+    residual_copy = coarse_copy(1)
+
+    perm_wide = jnp.concatenate([perm, perm], axis=1)
     for f in range(5):
-        coarse(0, f, sums(u0[5] * u1[f]) * inv, cs_ref)
-    state_copy = coarse_copy(0)
-
-    interior(u1, False)
-
-    boundary(2, copies2, False)
-    for f in range(5):
-        coarse(1, f, sums(res[f]), cr_ref)
-    residual_copy = coarse_copy(1)
-
-    for f in range(5):
-        flat = u1[f].reshape(256, LANES)
-        back = sum(dot(perm, part, ((1,), (1,))) for part in pieces(flat))
+        hi, mid, _ = pieces(u1[f].reshape(256, LANES))
+        back = dot(perm_wide, jnp.concatenate([hi, mid], axis=1), ((1,), (1,)))
         fine_ref[f, :, 0:256] = back[0:brick]
         fine_ref[f, :, 256:512] = back[brick:2 * brick]
 
     coarse_finish(0, state_copy, cs_ref)
     coarse_finish(1, residual_copy, cr_ref)
+
+
+def write_out(*refs):
+    sources, targets, sem = refs[:3], refs[3:6], refs[6]
+    copies = [pltpu.make_async_copy(sources[i], targets[i], sem.at[i]) for i in range(3)]
+    for copy in copies:
+        copy.start()
+    for copy in copies:
+        copy.wait()
 
 
 def local(n, state, volume, neighbour, parent):
     brick = state.shape[1]
     grid = (4, 8, 8, LANES)
     vmem = pl.BlockSpec(memory_space=pltpu.VMEM)
+    hbm = pl.BlockSpec(memory_space=pltpu.HBM)
     coarse_shape = jax.ShapeDtypeStruct((5, brick // 8, BE ** 3), f32)
-    return pl.pallas_call(
+    shapes = (jax.ShapeDtypeStruct(state.shape, f32), coarse_shape, coarse_shape)
+    held = pl.pallas_call(
         functools.partial(kernel, n),
-        out_shape=(jax.ShapeDtypeStruct(state.shape, f32), coarse_shape, coarse_shape),
-        in_specs=[vmem] * 4,
+        out_shape=tuple(pltpu.VMEM(one.shape, one.dtype) for one in shapes),
+        in_specs=[hbm, vmem, vmem, hbm],
         out_specs=(vmem,) * 3,
         scratch_shapes=[
+            pltpu.VMEM(volume.shape, i32),
+            pltpu.VMEM(state.shape, f32),
+            pltpu.SemaphoreType.DMA((6,)),
             pltpu.VMEM((6,) + grid, f32),
             pltpu.VMEM((5,) + grid, f32),
             pltpu.VMEM((5,) + grid, f32),
             pltpu.VMEM(grid, f32),
             pltpu.VMEM((5,) + grid, f32),
             pltpu.VMEM(grid, f32),
-            pltpu.VMEM((8, LANES), f32),
             pltpu.VMEM((3, 6, 6, 8, LANES), f32),
             pltpu.VMEM((3, 6, 6, 8, LANES), f32),
             pltpu.VMEM((2, 5, 32, LANES), f32),
@@ -459,8 +486,16 @@
             pltpu.SemaphoreType.DMA((2,)),
         ],
         compiler_params=pltpu.CompilerParams(
-            collective_id=0, has_side_effects=True, vmem_limit_bytes=40 * 1024 * 1024),
-    )(volume, neighbour, parent.reshape(1, brick), state)
+            collective_id=0, has_side_effects=True, vmem_limit_bytes=60 * 1024 * 1024),
+    )(volume, neighbour.T, parent.reshape(1, brick), state)
+    return pl.pallas_call(
+        write_out,
+        out_shape=shapes,
+        in_specs=[vmem] * 3,
+        out_specs=(hbm,) * 3,
+        scratch_shapes=[pltpu.SemaphoreType.DMA((3,))],
+        compiler_params=pltpu.CompilerParams(vmem_limit_bytes=4 * 1024 * 1024),
+    )(*held)
 
 
 def solution(mesh):

time: 32.1 us -> 27.6 us (0.86)
  local copies, waits for them, and re-layouts: 4.88 us -> 0 us
  Pallas kernels: 26.3 us -> 26.8 us
    unnamed x10 -> x0, local copies, waits for them, and re-layouts: 4.88 us -> none
    pallas_call x1 -> x2, Pallas kernels: 26.3 us -> 26.8 us  [the longest x1 25.9 us: local(): pl.pallas_call(functools.partial(kernel, n), out_shape=tuple((pltpu.VMEM(...]
where the time goes in v1:
time: 27.6 us; the launch traced here: 27.4 us
  Pallas kernels  26.8 us (97%)
  between operations  0.64 us (2%)
    pallas_call x1, Pallas kernels, local(): pl.pallas_call(functools.partial(kernel, n), out_shape=tuple((pltpu.VMEM(...  25.9 us
    pallas_call x1, Pallas kernels, local(): pl.pallas_call(write_out, out_shape=shapes, in_specs=[vmem] * 3, out_spec...  0.91 us

profile of v1, /device:TPU:0, one launch (start us, length us, event | category | flops | bytes accessed | tf_op | source)
XLA Modules:
  0.0 27.4 jit_solution(2852525670818384432)
XLA Ops:
  0.6 25.9 %shard_map.67 = (f32[5,64,512]{2,1,0:T(8,128)S(1)}, f32[5,8,512]{2,1,0:T(8,128)S(1)}, f32[5,8,512]{2,1,0:T(8,128)S(1)}) custom-call(s32[64,512]{1,0:T(8,128)} %vol_hbm.1, s32[6,64]{1,0:T(8,128)} %bitcast.2, s32[1,64]{1,0:T(1,128)} %bitcast.3, f32[5,64,512]{2,1,0:T(8,128)} %x_hbm.1), custom_call_target="tpu_custom_call" | custom-call | tf_op jit(solution)/shard_map/pallas_call | solution.py:464
  26.5 0.9 %shard_map.68 = (f32[5,64,512]{2,1,0:T(8,128)}, f32[5,8,512]{2,1,0:T(8,128)}, f32[5,8,512]{2,1,0:T(8,128)}) custom-call(f32[5,64,512]{2,1,0:T(8,128)S(1)} %get-tuple-element.6.refs_0_, f32[5,8,512]{2,1,0:T(8,128)S(1)} %get-tuple-element.7.refs_1_, f32[5,8,512]{2,1,0:T(8,128)S(1)} %get-tuple-element.8.refs_2_), custom_call_target="tpu_custom_call" | custom-call | tf_op jit(solution)/shard_map/pallas_call | solution.py:491

commit v2 on v1

--- a/solution.py
+++ b/solution.py
@@ -194,17 +194,18 @@
         return v
 
     def exchange(stage, src):
-        copies = []
         count = 6 if stage == 0 else 5
-        for k in range(3):
-            for high in (0, 1):
-                face_index = 2 * k + high
-                send[stage, face_index, 0:count] = pack(src, count, k, high)
         if stage == 0:
+            for k in (1, 0, 2):
+                for high in (0, 1):
+                    send[stage, 2 * k + high, 0:count] = pack(src, count, k, high)
             pl.semaphore_wait(barrier, 8)
-        for k in range(3):
+        copies = {}
+        for k in (1, 0, 2):
             for high in (0, 1):
                 mine = 2 * k + high
+                if stage > 0:
+                    send[stage, mine, 0:count] = pack(src, count, k, high)
                 copy = pltpu.make_async_remote_copy(
                     src_ref=send.at[stage, mine, pl.ds(0, count)],
                     dst_ref=recv.at[stage, 2 * k + 1 - high, pl.ds(0, count)],
@@ -213,9 +214,25 @@
                     device_id=((above if high else below)[k],),
                     device_id_type=MESH,
                 )
-                copy.start()
-                copies.append(copy)
+                copies[mine] = copy
+                if k == 1:
+                    copy.start()
+                else:
+                    pl.when(jnp.logical_not(at_end(k, high)))(copy.start)
+        for k in (0, 2):
+            for high in (0, 1):
+                index = 2 * k + high
+
+                @pl.when(at_end(k, high))
+                def _():
+                    for f in range(5):
+                        recv[stage, index, f] = jnp.full((8, LANES), STREAM[f], f32)
+                    if stage == 0:
+                        recv[stage, index, 5] = send[stage, index, 5]
         return copies
+
+    def at_end(k, high):
+        return coord[k] == (extent[k] - 1 if high else 0)
 
     def shift_x(a):
         return jnp.concatenate([a[1:4], roll(a[0:1], -16, 2)], axis=0)
@@ -265,7 +282,7 @@
                 lam[:, y] = spread
             return carry
 
-        lax.fori_loop(0, 8, pass_xz, 0)
+        lax.fori_loop(0, 8, pass_xz, 0, unroll=True)
 
         def pass_y(x, carry):
             u = [src[f, x] for f in range(5)]
@@ -281,11 +298,16 @@
                 lam[x] = lam[x] + (s + back_y(s))
             return carry
 
-        lax.fori_loop(0, 4, pass_y, 0)
+        lax.fori_loop(0, 4, pass_y, 0, unroll=True)
 
     def boundary(stage, copies, want_lam):
-        for copy in copies:
-            copy.wait()
+        for k in (0, 2, 1):
+            for high in (0, 1):
+                if k == 1:
+                    copies[2 * k + high].wait()
+                else:
+                    pl.when(jnp.logical_not(at_end(k, high)))(copies[2 * k + high].wait_send)
+                    pl.when(jnp.logical_not(at_end(k, 1 - high)))(copies[2 * k + high].wait_recv)
         for k in range(3):
             for high in (0, 1):
                 index = 2 * k + high
@@ -293,10 +315,6 @@
                 own_a = send[0, index, 5]
                 other_u = [recv[stage, index, f] for f in range(5)]
                 other_a = recv[0, index, 5]
-                if k != 1:
-                    at_end = coord[k] == (extent[k] - 1 if high else 0)
-                    other_u = [jnp.where(at_end, STREAM[f], other_u[f]) for f in range(5)]
-                    other_a = jnp.where(at_end, own_a, other_a)
                 if high:
                     w, s = face_from(own_u, own_a, other_u, other_a, k)
                     sign = 1.0
@@ -335,12 +353,12 @@
         def first(y, carry):
             box[0, :, y] = box_z(box_x(u0[5, :, y]))
             return carry
-        lax.fori_loop(0, 8, first, 0)
+        lax.fori_loop(0, 8, first, 0, unroll=True)
 
         def second(x, carry):
             gain[x] = (1.0 - u0[5, x]) / box_y(box[0, x])
             return carry
-        lax.fori_loop(0, 4, second, 0)
+        lax.fori_loop(0, 4, second, 0, unroll=True)
 
     def update(factor):
         def first(y, carry):
@@ -350,14 +368,14 @@
                 res[f, :, y] = d
                 box[f, :, y] = box_z(box_x(d))
             return carry
-        lax.fori_loop(0, 8, first, 0)
+        lax.fori_loop(0, 8, first, 0, unroll=True)
 
         def second(x, carry):
             g = gain[x]
             for f in range(5):
                 u1[f, x] = u0[f, x] + factor * (res[f, x] + g * box_y(box[f, x]))
             return carry
-        lax.fori_loop(0, 4, second, 0)
+        lax.fori_loop(0, 4, second, 0, unroll=True)
 
     copies0 = exchange(0, u0)
     box_of_frac()
@@ -372,12 +390,27 @@
 
     copies2 = exchange(2, u1)
 
-    r = iota((64, LANES), 0)
-    ln = iota((64, LANES), 1)
-    coarse_base = jnp.where(r >= 32, nxt, me) * (brick // 8)
-    pick = ((((r >> 3) & 3) == ((ln >> 4) & 3))
-            & (jnp.broadcast_to(par_lane >> 3, (64, LANES)) == coarse_base + (r & 7)))
-    pick = jnp.where(pick, 1.0, 0.0).astype(bf16)
+    coarse_count = brick // 8
+    slot = par_lane >> 3
+    slots = iota((coarse_count, LANES), 0)
+    kept = jnp.where(slot == me * coarse_count + slots, 1.0, 0.0)
+    sent = jnp.where(slot == nxt * coarse_count + slots, 1.0, 0.0)
+    some_sent = jnp.max(sent, axis=1, keepdims=True)
+    sent_before = jnp.sum(jnp.where(slots < slot - nxt * coarse_count, some_sent, 0.0),
+                          axis=0, keepdims=True).astype(i32)
+    goes = jnp.max(sent, axis=0, keepdims=True) > 0.5
+    missing = 1.0 - jnp.max(kept, axis=1, keepdims=True)
+    sq_row = iota((coarse_count, coarse_count), 0)
+    sq_col = iota((coarse_count, coarse_count), 1)
+    missing_row = jnp.sum(jnp.where(sq_row == sq_col, missing, 0.0), axis=0, keepdims=True)
+    missing_before = jnp.sum(jnp.where(sq_col < sq_row, missing_row, 0.0),
+                             axis=1, keepdims=True).astype(i32)
+    r = iota((48, LANES), 0)
+    ln = iota((48, LANES), 1)
+    tile = (ln >> 4) & 3
+    own_row = jnp.where((tile == (r >> 3)) & (slot == me * coarse_count + (r & 7)), 1.0, 0.0)
+    sent_row = jnp.where((tile == ((r - 32) >> 2)) & (sent_before == (r & 3)) & goes, 1.0, 0.0)
+    pick = jnp.where(r < 32, own_row, sent_row).astype(bf16)
     pick2 = jnp.concatenate([pick, pick], axis=1)
     lane_oy, lane_oz = (lane >> 2) & 1, lane & 1
     sub = iota((1, 8, LANES), 1)
@@ -405,7 +438,7 @@
         placed = dot(pick2, jnp.concatenate([hi, mid], axis=1), ((1,), (1,)))
         for f in range(5):
             block = placed[:, f * LANES:(f + 1) * LANES]
-            csend[group, f] = block[32:64]
+            csend[group, f] = block[32:48]
             for t in range(4):
                 out[f, :, t * LANES:(t + 1) * LANES] = block[8 * t:8 * t + 8]
 
@@ -422,7 +455,12 @@
         for f in range(5):
             for t in range(4):
                 at = (f, slice(None), slice(t * LANES, (t + 1) * LANES))
-                out[at] = out[at] + crecv[group, f, 8 * t:8 * t + 8]
+                arrived = crecv[group, f, 4 * t:4 * t + 4]
+                total = out[at]
+                for rank in range(4):
+                    here = (missing > 0.5) & (missing_before == rank)
+                    total = jnp.where(here, arrived[rank:rank + 1], total)
+                out[at] = total
 
     inv = 1.0 / sums(u0[5])
     coarse(0, [sums(u0[5] * u1[f]) * inv for f in range(5)], cs_ref)
@@ -478,8 +516,8 @@
             pltpu.VMEM(grid, f32),
             pltpu.VMEM((3, 6, 6, 8, LANES), f32),
             pltpu.VMEM((3, 6, 6, 8, LANES), f32),
-            pltpu.VMEM((2, 5, 32, LANES), f32),
-            pltpu.VMEM((2, 5, 32, LANES), f32),
+            pltpu.VMEM((2, 5, 16, LANES), f32),
+            pltpu.VMEM((2, 5, 16, LANES), f32),
             pltpu.SemaphoreType.DMA((3, 6)),
             pltpu.SemaphoreType.DMA((3, 6)),
             pltpu.SemaphoreType.DMA((2,)),

time: 27.6 us -> 24.7 us (0.89)
  Pallas kernels: 26.8 us -> 23.9 us
    pallas_call x1, Pallas kernels: 25.9 us -> 23 us  [local(): pl.pallas_call(functools.partial(kernel, n), out_shape=tuple((pltpu.VMEM(...]
where the time goes in v2:
time: 24.7 us; the launch traced here: 24.6 us
  Pallas kernels  23.9 us (97%)
  between operations  0.64 us (3%)
    pallas_call x1, Pallas kernels, local(): pl.pallas_call(functools.partial(kernel, n), out_shape=tuple((pltpu.VMEM(...  23 us
    pallas_call x1, Pallas kernels, local(): pl.pallas_call(write_out, out_shape=shapes, in_specs=[vmem] * 3, out_spec...  0.91 us

profile of v2, /device:TPU:0, one launch (start us, length us, event | category | flops | bytes accessed | tf_op | source)
XLA Modules:
  0.0 24.6 jit_solution(10257957015340296887)
XLA Ops:
  0.6 23.0 %shard_map.67 = (f32[5,64,512]{2,1,0:T(8,128)S(1)}, f32[5,8,512]{2,1,0:T(8,128)S(1)}, f32[5,8,512]{2,1,0:T(8,128)S(1)}) custom-call(s32[64,512]{1,0:T(8,128)} %vol_hbm.1, s32[6,64]{1,0:T(8,128)} %bitcast.2, s32[1,64]{1,0:T(1,128)} %bitcast.3, f32[5,64,512]{2,1,0:T(8,128)} %x_hbm.1), custom_call_target="tpu_custom_call" | custom-call | tf_op jit(solution)/shard_map/pallas_call | solution.py:502
  23.7 0.9 %shard_map.68 = (f32[5,64,512]{2,1,0:T(8,128)}, f32[5,8,512]{2,1,0:T(8,128)}, f32[5,8,512]{2,1,0:T(8,128)}) custom-call(f32[5,64,512]{2,1,0:T(8,128)S(1)} %get-tuple-element.6.refs_0_, f32[5,8,512]{2,1,0:T(8,128)S(1)} %get-tuple-element.7.refs_1_, f32[5,8,512]{2,1,0:T(8,128)S(1)} %get-tuple-element.8.refs_2_), custom_call_target="tpu_custom_call" | custom-call | tf_op jit(solution)/shard_map/pallas_call | solution.py:529

commit v3 on v2

--- a/solution.py
+++ b/solution.py
@@ -462,11 +462,11 @@
                     total = jnp.where(here, arrived[rank:rank + 1], total)
                 out[at] = total
 
+    interior(u1, False)
+
     inv = 1.0 / sums(u0[5])
     coarse(0, [sums(u0[5] * u1[f]) * inv for f in range(5)], cs_ref)
     state_copy = coarse_copy(0)
-
-    interior(u1, False)
 
     boundary(2, copies2, False)
     coarse(1, [sums(res[f]) for f in range(5)], cr_ref)

time: 24.7 us -> 24.8 us (level)
  no operation moved by 1% of the time
where the time goes in v3:
time: 24.8 us; the launch traced here: 24.6 us
  Pallas kernels  23.9 us (96%)
  between operations  0.64 us (3%)
    pallas_call x1, Pallas kernels, local(): pl.pallas_call(functools.partial(kernel, n), out_shape=tuple((pltpu.VMEM(...  23 us
    pallas_call x1, Pallas kernels, local(): pl.pallas_call(write_out, out_shape=shapes, in_specs=[vmem] * 3, out_spec...  0.91 us

profile of v3, /device:TPU:0, one launch (start us, length us, event | category | flops | bytes accessed | tf_op | source)
XLA Modules:
  0.0 24.6 jit_solution(16644095844510334289)
XLA Ops:
  0.6 23.0 %shard_map.67 = (f32[5,64,512]{2,1,0:T(8,128)S(1)}, f32[5,8,512]{2,1,0:T(8,128)S(1)}, f32[5,8,512]{2,1,0:T(8,128)S(1)}) custom-call(s32[64,512]{1,0:T(8,128)} %vol_hbm.1, s32[6,64]{1,0:T(8,128)} %bitcast.2, s32[1,64]{1,0:T(1,128)} %bitcast.3, f32[5,64,512]{2,1,0:T(8,128)} %x_hbm.1), custom_call_target="tpu_custom_call" | custom-call | tf_op jit(solution)/shard_map/pallas_call | solution.py:502
  23.7 0.9 %shard_map.68 = (f32[5,64,512]{2,1,0:T(8,128)}, f32[5,8,512]{2,1,0:T(8,128)}, f32[5,8,512]{2,1,0:T(8,128)}) custom-call(f32[5,64,512]{2,1,0:T(8,128)S(1)} %get-tuple-element.6.refs_0_, f32[5,8,512]{2,1,0:T(8,128)S(1)} %get-tuple-element.7.refs_1_, f32[5,8,512]{2,1,0:T(8,128)S(1)} %get-tuple-element.8.refs_2_), custom_call_target="tpu_custom_call" | custom-call | tf_op jit(solution)/shard_map/pallas_call | solution.py:529
